TPU v7x, 512 devices: a whole 4x8x8 slice. The times are simulated.
512 devices in a mesh: sweep: 8 (over z_lo, core), recv: 64 (over x, y, z_hi).
Axes of the slice: x: 4, y: 8, z: 8 (z_hi: 2, z_lo: 4; z = z_hi * 4 + z_lo), core: 2. Of those that a mesh axis runs over, the one named last changes fastest.
Arguments:
- records: bfloat16 [16, 4096, 4096], P('sweep', 'recv'), may hold values from -6 to 6
- pilots: bfloat16 [16, 3968], replicated, may hold values from -0.09375 to 0.09375
- hadamard: int32 [16, 16], replicated, may hold values from -1 to 1, as said below
- code_vibrator: int32 [16], replicated, may hold values from 0 to 15, each once
- owner_map: int32 [4096], P('recv'), may hold values from 0 to 15
- live_mask: int32 [4096], P('recv'), may hold values 0 or 1
- filters: bfloat16 [16, 128, 128], P('sweep'), may hold values from -0.5 to 0.5
- targets: bfloat16 [16, 4096, 128], P('sweep', 'recv'), may hold values from -6 to 6
Outputs:
- responses: float32 [16, 4096, 128], P('sweep', 'recv')
- gradient: float32 [16, 128, 128], P('sweep', 'recv')
Inputs may be any that keep to these rules, and one draw needn't show every extreme that they name: hadamard transposed times hadamard is 16 times the identity. `code_vibrator`: every vibrator belongs to exactly one code.
All inputs are finite; a program needn't handle non-finite values. No bound on the sum of `live_mask` on one device may be relied on, other than what follows from the above.
Results may differ from a plain program's by a relative error of at most 0.0085.
Values may be sent and summed in bfloat16 or wider, within the bound.
A program may use at most 64 MiB of HBM per device.

v0:
```python
import math
import jax
import jax.numpy as jnp
from jax import lax
from jax.sharding import PartitionSpec as P


def toeplitz(sweep_pilot, samples, lagcount):
    padding = jnp.zeros((samples + 1 - sweep_pilot.shape[0],), sweep_pilot.dtype)
    extended = jnp.concatenate([sweep_pilot, padding])
    return jnp.tile(extended, lagcount)[: lagcount * samples].reshape(lagcount, samples)


def correlate_split(combined, sweep_pilot, samples, lagcount):
    upper = combined.astype(jnp.bfloat16)
    lower = (combined - upper.astype(jnp.float32)).astype(jnp.bfloat16)
    paired = jnp.concatenate([upper, lower], axis=0)
    toe_rows = toeplitz(sweep_pilot, samples, lagcount)
    lagged = lax.dot_general(
        paired, toe_rows, (((1,), (1,)), ((), ())), preferred_element_type=jnp.float32
    )
    half = combined.shape[0]
    return lagged[:half] + lagged[half:]


def local(records, pilots, hadamard, code_vibrator, owner_map, live_mask, filters, targets):
    codes = hadamard.shape[1]
    held_sweeps = records.shape[0]
    channels = records.shape[1]
    samples = records.shape[2]
    lagcount = filters.shape[1]
    owned_codes = filters.shape[0]
    first_code = lax.axis_index("sweep") * owned_codes
    code_norm = 1.0 / math.sqrt(codes)
    onehot = (code_vibrator[:, None] == jnp.arange(codes, dtype=jnp.int32)[None, :]).astype(
        jnp.bfloat16
    )
    code_pilot = jnp.dot(onehot, pilots, preferred_element_type=jnp.float32).astype(jnp.bfloat16)
    sign_table = hadamard.astype(jnp.bfloat16)
    sign_rows = lax.dynamic_slice_in_dim(
        sign_table, lax.axis_index("sweep") * held_sweeps, held_sweeps, 0
    )

    def column(operands):
        sweep_pilot, signs_col = operands
        combined = jnp.einsum("s,srt->rt", signs_col, records, preferred_element_type=jnp.float32)
        return code_norm * correlate_split(combined, sweep_pilot, samples, lagcount)

    decoded = lax.psum_scatter(
        lax.map(column, (code_pilot, sign_rows.T)), "sweep", scatter_dimension=0, tiled=True
    ).astype(jnp.bfloat16)
    col_vibs = lax.dynamic_slice_in_dim(code_vibrator, first_code, owned_codes, 0)
    responses = jnp.einsum("crl,clm->crm", decoded, filters, preferred_element_type=jnp.float32)
    owned = (owner_map[None, :] == col_vibs[:, None]).astype(jnp.float32)
    weight = live_mask.astype(jnp.float32)[None, :] * (0.25 + owned)
    residual = (weight[:, :, None] * (responses - targets.astype(jnp.float32))).astype(jnp.bfloat16)
    factor = 1.0 / math.sqrt(channels * lax.axis_size("recv"))
    local_grad = (
        jnp.einsum("crl,crm->clm", decoded, residual, preferred_element_type=jnp.float32) * factor
    )
    summed = lax.psum(local_grad, "recv")
    share_rows = lagcount // lax.axis_size("recv")
    gradient = lax.dynamic_slice_in_dim(summed, lax.axis_index("recv") * share_rows, share_rows, 1)
    return (responses, gradient)


def solution(mesh):
    in_specs = (
        P("sweep", "recv", None),
        P(),
        P(),
        P(),
        P("recv"),
        P("recv"),
        P("sweep", None, None),
        P("sweep", "recv", None),
    )
    out_specs = (P("sweep", "recv", None), P("sweep", "recv", None))
    return jax.shard_map(local, mesh=mesh, in_specs=in_specs, out_specs=out_specs, check_vma=False)
```

profile of v0, /device:TPU:8, one launch (start us, length us, event | category | flops | bytes accessed | tf_op | source)
XLA Modules:
  0.0 939.9 jit_solution(15561842590453519801)
XLA Ops:
  8.1 0.9 convolution_convert_fusion
  9.0 97.8 %while.10 = (s32[]{:T(128)}, f32[16,64,128]{2,1,0:T(8,128)}, bf16[16,2]{1,0:T(8,128)(2,1)S(1)}, bf16[2,64,4096]{2,1,0:T(8,128)(2,1)}, bf16[16,3968]{1,0:T(8,128)(2,1)S(1)}, /*index=5*/s32[]{:T(128)}, bf16[]{:T(256)}) while((s32[]{:T(128)}, f32[16,64,128]{2,1,0:T(8,128)}, bf16[16,2]{1,0:T(8,128)(2,1)S(1)}, bf16[2,64,4096]{2,1,0:T(8,128)(2,1)}, ...), condition=%wide.region_1.2_spmd, body=%wide.region_0.1_spmd.sunk | while | flops 138428416 | bytes 19079812 | solution.py:50
  9.2 1.1 tile.12
  10.9 0.7 copy-done.6
  11.6 1.3 fusion.35
  15.3 1.1 tile.12
  17.0 0.7 copy-done.6
  17.8 1.3 fusion.35
  21.4 1.1 tile.12
  23.2 0.7 copy-done.6
  23.9 1.3 fusion.35
  27.5 1.1 tile.12
  29.3 0.7 copy-done.6
  30.0 1.3 fusion.35
  33.6 1.1 tile.12
  35.4 0.7 copy-done.6
  36.1 1.3 fusion.35
  39.8 1.1 tile.12
  42.2 1.3 fusion.35
  45.9 1.1 tile.12
  47.6 0.7 copy-done.6
  48.3 1.3 fusion.35
  52.0 1.1 tile.12
  53.7 0.7 copy-done.6
  54.4 1.3 fusion.35
  58.1 1.1 tile.12
  59.8 0.7 copy-done.6
  60.6 1.3 fusion.35
  64.2 1.1 tile.12
  66.7 1.3 fusion.35
  70.3 1.1 tile.12
  72.8 1.3 fusion.35
  76.5 1.1 tile.12
  78.9 1.3 fusion.35
  82.6 1.1 tile.12
  85.0 1.3 fusion.35
  88.7 1.1 tile.12
  91.1 1.3 fusion.35
  94.8 1.1 tile.12
  96.5 0.7 copy-done.6
  97.2 1.3 fusion.35
  100.9 1.1 tile.12
  103.4 1.3 fusion.35
  107.1 43.9 %reduce-scatter.2.cloned.1.call-done = f32[2,64,128]{2,1,0:T(8,128)} async-done(((f32[16,64,128]{2,1,0:T(8,128)}), f32[2,64,128]{2,1,0:T(8,128)}) %reduce-scatter.2.cloned.1.call-update) | async-done | bytes 65552 | tf_op jit(solution)/shard_map/reduce_scatter | solution.py:49
  151.0 1.0 fusion.15
  152.0 1.8 convolution_multiply_fusion
  153.8 778.0 %all-reduce.3.cloned.1.call-done = f32[2,128,128]{2,1,0:T(8,128)} async-done(((f32[2,128,128]{2,1,0:T(8,128)}), f32[2,128,128]{2,1,0:T(8,128)}) %all-reduce.3.cloned.1.call-update) | async-done | bytes 131088 | tf_op jit(solution)/shard_map/psum | solution.py:61
  931.8 1.3 constant_dynamic-slice_fusion.1
  (192 shorter events, 53.0 us)
Async XLA Ops:
  7.2 0.9 copy-start
  7.2 143.8 %reduce-scatter.2.cloned.1.call-start = ((), (), s32[]{:S(2)}) async-start(), calls=%async_computation.1 | async-start | bytes 589824 | tf_op jit(solution)/shard_map/reduce_scatter | solution.py:49
  9.0 98.0 %copy-start.4 = (s32[16]{0:T(128)S(1)}, s32[16]{0:T(128)}, u32[]{:S(2)}) copy-start(s32[16]{0:T(128)} %param.13) | copy-start | bytes 196
  9.0 98.1 %copy-start.7 = (s32[64]{0:T(128)S(1)}, s32[64]{0:T(128)}, u32[]{:S(2)}) copy-start(s32[64]{0:T(128)} %param.15) | copy-start | bytes 772
  9.0 98.1 %copy-start.5 = (s32[64]{0:T(128)S(1)}, s32[64]{0:T(128)}, u32[]{:S(2)}) copy-start(s32[64]{0:T(128)} %param.14) | copy-start | bytes 772
  9.0 142.0 %copy-start.2 = (bf16[2,128,128]{2,1,0:T(8,128)(2,1)S(1)}, bf16[2,128,128]{2,1,0:T(8,128)(2,1)}, u32[]{:S(2)}) copy-start(bf16[2,128,128]{2,1,0:T(8,128)(2,1)} %param.16) | copy-start | bytes 196612
  9.0 143.0 %copy-start.3 = (bf16[2,64,128]{2,1,0:T(8,128)(2,1)S(1)}, bf16[2,64,128]{2,1,0:T(8,128)(2,1)}, u32[]{:S(2)}) copy-start(bf16[2,64,128]{2,1,0:T(8,128)(2,1)} %param.17) | copy-start | bytes 98308
  10.4 1.2 copy-start.6
  16.5 1.2 copy-start.6
  22.6 1.2 copy-start.6
  28.8 1.2 copy-start.6
  34.9 1.2 copy-start.6
  41.0 1.2 copy-start.6
  47.1 1.2 copy-start.6
  53.2 1.2 copy-start.6
  59.3 1.2 copy-start.6
  65.4 1.2 copy-start.6
  71.6 1.2 copy-start.6
  77.7 1.2 copy-start.6
  83.8 1.2 copy-start.6
  89.9 1.2 copy-start.6
  96.0 1.2 copy-start.6
  102.1 1.2 copy-start.6
  106.9 824.9 %all-reduce.3.cloned.1.call-start = ((), (), s32[]{:S(2)}) async-start(), calls=%async_computation.2 | async-start | bytes 262144 | tf_op jit(solution)/shard_map/psum | solution.py:61
  152.0 781.1 %copy-start.1 = (f32[2,64,128]{2,1,0:T(8,128)}, f32[2,64,128]{2,1,0:T(8,128)S(1)}, u32[]{:S(2)}) copy-start(f32[2,64,128]{2,1,0:T(8,128)S(1)} %fusion.15) | copy-start | bytes 196612
Sparse Core Ops, SparseCore 0:
  107.0 43.9 reduce-scatter.1
  154.2 777.6 all-reduce.2
where the time goes:
time: 941 us; the launch traced here: 940 us
  waiting for transfers between devices  822 us (87%)
  local copies, waits for them, and re-layouts  52.6 us (6%)
  matrix products  30.8 us (3%)
  other arithmetic  19.3 us (2%)
  between operations  14.1 us (1%)
    psum x1, waiting for transfers between devices, local(): summed = lax.psum(local_grad, 'recv')  778 us
    reduce_scatter x1, waiting for transfers between devices, local(): lax.psum_scatter(lax.map(column, (code_pilot, sign_rows.T)), 'sweep', sca...  43.9 us
    dot_general x16, matrix products, column(): jnp.einsum('s,srt->rt', signs_col, records, preferred_element_type=jnp.fl...  20.2 us
    another operation x32, local copies, waits for them, and re-layouts, toeplitz(): jnp.tile(extended, lagcount)[:lagcount * samples].reshape(lagcount, samples)  19.6 us
  transfers between devices with their start and end apart: 2, of which 2 were waited for; matrix products, arithmetic and copies ran while one was open for 0% of the time, Pallas kernels for 0%

commit v1 on v0

--- a/solution.py
+++ b/solution.py
@@ -3,6 +3,11 @@
 import jax.numpy as jnp
 from jax import lax
 from jax.sharding import PartitionSpec as P
+
+
+def summed_here(value, axis):
+    blocks = lax.all_gather(value, axis)
+    return jnp.sum(blocks, axis=0)
 
 
 def toeplitz(sweep_pilot, samples, lagcount):
@@ -58,7 +63,7 @@
     local_grad = (
         jnp.einsum("crl,crm->clm", decoded, residual, preferred_element_type=jnp.float32) * factor
     )
-    summed = lax.psum(local_grad, "recv")
+    summed = summed_here(local_grad, "recv")
     share_rows = lagcount // lax.axis_size("recv")
     gradient = lax.dynamic_slice_in_dim(summed, lax.axis_index("recv") * share_rows, share_rows, 1)
     return (responses, gradient)

time: 941 us -> 375 us (0.40)
  the two profiles are of different devices: /device:TPU:8 before, /device:TPU:2 now
where the time goes in v1:
time: 375 us; the launch traced here: 374 us
  waiting for transfers between devices  245 us (65%)
  matrix products  50.3 us (13%)
  local copies, waits for them, and re-layouts  40.4 us (11%)
  other arithmetic  22.9 us (6%)
  between operations  14.1 us (4%)
    all_gather x1, waiting for transfers between devices, summed_here(): blocks = lax.all_gather(value, axis)  202 us
    reduce_scatter x1, waiting for transfers between devices, local(): lax.psum_scatter(lax.map(column, (code_pilot, sign_rows.T)), 'sweep', sca...  43.9 us
    dot_general x16, matrix products, column(): jnp.einsum('s,srt->rt', signs_col, records, preferred_element_type=jnp.fl...  39.8 us
    another operation x32, local copies, waits for them, and re-layouts, toeplitz(): jnp.tile(extended, lagcount)[:lagcount * samples].reshape(lagcount, samples)  19.6 us
    dynamic_update_slice x16, other arithmetic, local(): lax.map(column, (code_pilot, sign_rows.T))  9.82 us
    convert_element_type x16, other arithmetic, correlate_split(): lower = (combined - upper.astype(jnp.float32)).astype(jnp.bfloat16)  9.22 us
    dot_general x16, local copies, waits for them, and re-layouts, column(): jnp.einsum('s,srt->rt', signs_col, records, preferred_element_type=jnp.fl...  9.18 us
    reshape x16, local copies, waits for them, and re-layouts, toeplitz(): jnp.tile(extended, lagcount)[:lagcount * samples].reshape(lagcount, samples)  7.9 us
  transfers between devices with their start and end apart: 2, of which 2 were waited for; matrix products, arithmetic and copies ran while one was open for 0% of the time, Pallas kernels for 0%

profile of v1, /device:TPU:2, one launch (start us, length us, event | category | flops | bytes accessed | tf_op | source)
XLA Modules:
  0.0 374.3 jit_solution(11026480520958797524)
XLA Ops:
  7.2 0.7 constant_dynamic-slice_fusion.2
  8.1 0.9 convolution_convert_fusion
  9.0 105.6 %while.10 = (s32[]{:T(128)}, f32[16,64,128]{2,1,0:T(8,128)}, bf16[16,2]{1,0:T(8,128)(2,1)S(1)}, bf16[2,64,4096]{2,1,0:T(8,128)(2,1)}, bf16[16,3968]{1,0:T(8,128)(2,1)S(1)}, /*index=5*/s32[]{:T(128)}, bf16[]{:T(256)}) while((s32[]{:T(128)}, f32[16,64,128]{2,1,0:T(8,128)}, bf16[16,2]{1,0:T(8,128)(2,1)S(1)}, bf16[2,64,4096]{2,1,0:T(8,128)(2,1)}, ...), condition=%wide.region_1.2_spmd, body=%wide.region_0.1_spmd.sunk | while | flops 138428416 | bytes 14885479 | solution.py:55
  9.1 2.5 fusion.35
  12.8 1.1 tile.12
  15.0 0.6 fusion.38
  15.7 2.5 fusion.35
  19.4 1.1 tile.12
  22.3 2.5 fusion.35
  26.0 1.1 tile.12
  28.2 0.6 fusion.38
  28.9 2.5 fusion.35
  32.6 1.1 tile.12
  35.5 2.5 fusion.35
  39.2 1.1 tile.12
  41.4 0.6 fusion.38
  42.1 2.5 fusion.35
  45.8 1.1 tile.12
  48.7 2.5 fusion.35
  52.4 1.1 tile.12
  54.6 0.6 fusion.38
  55.3 2.5 fusion.35
  59.0 1.1 tile.12
  61.2 0.6 fusion.38
  61.9 2.5 fusion.35
  65.6 1.1 tile.12
  67.8 0.6 fusion.38
  68.5 2.5 fusion.35
  72.2 1.1 tile.12
  75.1 2.5 fusion.35
  78.8 1.1 tile.12
  81.7 2.5 fusion.35
  85.4 1.1 tile.12
  88.3 2.5 fusion.35
  92.0 1.1 tile.12
  94.9 2.5 fusion.35
  98.6 1.1 tile.12
  100.8 0.6 fusion.38
  101.5 2.5 fusion.35
  105.2 1.1 tile.12
  107.4 0.6 fusion.38
  108.1 2.5 fusion.35
  111.8 1.1 tile.12
  114.8 43.9 %reduce-scatter.2.cloned.1.call-done = f32[2,64,128]{2,1,0:T(8,128)} async-done(((f32[16,64,128]{2,1,0:T(8,128)}), f32[2,64,128]{2,1,0:T(8,128)}) %reduce-scatter.2.cloned.1.call-update) | async-done | bytes 65552 | tf_op jit(solution)/shard_map/reduce_scatter | solution.py:54
  158.7 1.0 fusion.15
  159.7 1.7 convolution_multiply_fusion
  161.5 201.5 %all-gather.3.cloned.1.call-done = f32[128,128,128]{2,1,0:T(8,128)} async-done(((f32[2,128,128]{2,1,0:T(8,128)}), f32[128,128,128]{2,1,0:T(8,128)}) %all-gather.3.cloned.1.call-update) | async-done | bytes 8388624 | tf_op jit(solution)/shard_map/all_gather | solution.py:9
  363.0 3.8 %reduce_sum.9 = f32[2,128,128]{2,1,0:T(8,128)S(1)} reduce(f32[64,2,128,128]{3,2,1,0:T(8,128)} %bitcast.34, f32[]{:T(128)} %constant.8.clone.1), dimensions={0}, to_apply=%region_3.4 | reduce | flops 2064384 | bytes 8519684 | tf_op jit(solution)/shard_map/reduce_sum | solution.py:10
  (161 shorter events, 42.6 us)
Async XLA Ops:
  7.2 0.9 copy-start
  7.2 151.5 %reduce-scatter.2.cloned.1.call-start = ((), (), s32[]{:S(2)}) async-start(), calls=%async_computation.1 | async-start | bytes 589824 | tf_op jit(solution)/shard_map/reduce_scatter | solution.py:54
  9.0 105.7 %copy-start.4 = (s32[16]{0:T(128)S(1)}, s32[16]{0:T(128)}, u32[]{:S(2)}) copy-start(s32[16]{0:T(128)} %param.13) | copy-start | bytes 196
  9.0 105.8 %copy-start.6 = (s32[64]{0:T(128)S(1)}, s32[64]{0:T(128)}, u32[]{:S(2)}) copy-start(s32[64]{0:T(128)} %param.15) | copy-start | bytes 772
  9.0 105.8 %copy-start.5 = (s32[64]{0:T(128)S(1)}, s32[64]{0:T(128)}, u32[]{:S(2)}) copy-start(s32[64]{0:T(128)} %param.14) | copy-start | bytes 772
  9.0 149.7 %copy-start.2 = (bf16[2,128,128]{2,1,0:T(8,128)(2,1)S(1)}, bf16[2,128,128]{2,1,0:T(8,128)(2,1)}, u32[]{:S(2)}) copy-start(bf16[2,128,128]{2,1,0:T(8,128)(2,1)} %param.16) | copy-start | bytes 196612
  9.0 150.7 %copy-start.3 = (bf16[2,64,128]{2,1,0:T(8,128)(2,1)S(1)}, bf16[2,64,128]{2,1,0:T(8,128)(2,1)}, u32[]{:S(2)}) copy-start(bf16[2,64,128]{2,1,0:T(8,128)(2,1)} %param.17) | copy-start | bytes 98308
  114.6 248.4 %all-gather.3.cloned.1.call-start = ((), (), s32[]{:S(2)}) async-start(), calls=%async_computation.2 | async-start | bytes 8519680 | tf_op jit(solution)/shard_map/all_gather | solution.py:9
  159.7 207.1 %copy-start.1 = (f32[2,64,128]{2,1,0:T(8,128)}, f32[2,64,128]{2,1,0:T(8,128)S(1)}, u32[]{:S(2)}) copy-start(f32[2,64,128]{2,1,0:T(8,128)S(1)} %fusion.15) | copy-start | bytes 196612
Sparse Core Ops, SparseCore 0:
  114.7 43.9 reduce-scatter.1
  164.0 198.9 all-gather.2
